TPU v7x, 32 devices: a whole 2x2x4 slice. The times are simulated.
32 devices in a mesh: nodes: 8 (over z, x), rep: 4 (over y, core).
Axes of the slice: x: 2, y: 2, z: 4, core: 2. Of those that a mesh axis runs over, the one named last changes fastest.
Arguments:
- node_input: bfloat16 [6144, 256], P(('rep', 'nodes')), may hold values from -16 to 16
- edge_feat: bfloat16 [12288, 256], P(('rep', 'nodes')), may hold values from -6 to 6
- graph_ids: int32 [6144], P(('rep', 'nodes')), may hold values from 0 to 1536, as said below
- edge_src: int32 [12288], P(('rep', 'nodes')), may hold values from 0 to 239, as said below
- edge_dst: int32 [12288], P(('rep', 'nodes')), may hold values from 0 to 191, as said below
- halo_send: int32 [1536], P(('rep', 'nodes')), may hold values from 0 to 191, as said below
- w_proj: bfloat16 [2, 256, 1024], replicated, may hold values from -0.375 to 0.375
- w_edge: bfloat16 [2, 256, 256], replicated, may hold values from -0.375 to 0.375
- w_qkv: bfloat16 [2, 256, 768], replicated, may hold values from -0.25 to 0.25
- w_out: bfloat16 [2, 256, 256], replicated, may hold values from -1.5 to 1.5
- w_up: bfloat16 [2, 256, 512], replicated, may hold values from -0.375 to 0.375
- w_down: bfloat16 [2, 512, 256], replicated, may hold values from -0.25 to 0.25
- norm_gain: float32 [2, 3, 256], replicated, may hold values from 0.5 to 1.5
- norm_shift: float32 [2, 3, 256], replicated, may hold values from -1.5 to 1.5
- cotangent: bfloat16 [6144, 256], P(('rep', 'nodes')), may hold values from -6 to 6
Outputs:
- out_act: float32 [6144, 256], P(('rep', 'nodes'))
- grad_input: float32 [6144, 256], P(('rep', 'nodes'))
- grad_proj: float32 [2, 256, 1024], replicated
- grad_edge: float32 [2, 256, 256], replicated
- grad_qkv: float32 [2, 256, 768], replicated
- grad_out: float32 [2, 256, 256], replicated
- grad_up: float32 [2, 256, 512], replicated
- grad_down: float32 [2, 512, 256], replicated
- grad_gain: float32 [2, 3, 256], replicated
- grad_shift: float32 [2, 3, 256], replicated
Inputs may be any that keep to these rules, and one draw needn't show every extreme that they name: `graph_ids`: nodes of one group attend to each other only where their graph ids are equal; ids of different groups are unrelated. `edge_src`: indexes the device's 192 nodes followed by the 24 rows received from the previous and the 24 rows from the next device along nodes; every one of these rows is the source of some edge. `edge_dst`: every node of a device is the target of at least one of its edges. `halo_send`: per device, 24 distinct rows for the previous neighbour, then 24 distinct rows for the next.
All inputs are finite; a program needn't handle non-finite values.
Results may differ from a plain program's by a relative error of at most 0.025.
Values may be sent and summed in bfloat16 or wider, within the bound.
A program may use at most 256 MiB of HBM per device.

v0:
```python
import functools
import math

import jax
import jax.numpy as jnp
from jax import lax
from jax.experimental import pallas as pl
from jax.experimental.pallas import tpu as pltpu
from jax.sharding import PartitionSpec as P

HEADS = 8
HEAD_DIM = 32
NEG = -1e30
NORM_EPS = 1e-05
GATE_EPS = 1e-06
F32, BF16, I32 = jnp.float32, jnp.bfloat16, jnp.int32
MESH = pl.DeviceIdType.MESH
SYNCS = 12
STRIP = 32
GROUPS = (
    ("early", 1, 0, 2560, ("core", "y", "nodes")),
    ("conv", 1, 0, 2560, ("core", "y", "nodes")),
    ("qkv", 1, 0, 1536, ("core", "y", "nodes")),
    ("early", 0, 0, 2560, ("core", "x", "y", "z")),
    ("conv", 0, 0, 2560, ("core", "y", "nodes")),
    ("qkv", 0, 0, 1024, ("rep", "nodes")),
    ("qkv", 0, 1024, 512, ("nodes", "rep")),
)


def dot(left, right):
    return lax.dot_general(
        left, right, (((1,), (0,)), ((), ())), preferred_element_type=F32
    )


def dot_nt(left, right):
    return lax.dot_general(
        left, right, (((1,), (1,)), ((), ())), preferred_element_type=F32
    )


def dot_tn(left, right):
    return lax.dot_general(
        left, right, (((0,), (0,)), ((), ())), preferred_element_type=F32
    )


def split(value):
    high = value.astype(BF16)
    return high, (value - high.astype(F32)).astype(BF16)


def sigmoid(value):
    return jax.nn.sigmoid(value)


def silu_slope(value):
    logistic = sigmoid(value)
    return logistic * (1.0 + value * (1.0 - logistic))


def col_sum(value):
    return jnp.sum(value, axis=0, keepdims=True)


def pack(first, second):
    return jnp.concatenate([first[:, :128], first[:, 128:], second[:, :128], second[:, 128:]], 0)


def unpack(tile):
    return [jnp.concatenate([tile[i : i + 1], tile[i + 1 : i + 2]], 1) for i in (0, 2)]


def combine_moments(tiles, count):
    mean = jnp.mean(tiles[:, 0:2], 0)
    off = tiles[:, 0:2] - mean
    return jnp.concatenate([mean, jnp.sum(tiles[:, 2:4] + count * off * off, 0)], 0)


class Refs:
    pass


def axis_sizes(N, M):
    return dict(core=2, y=M // 2, x=2, z=N // 2, rep=M, nodes=N)


def scratch_list(N, M, L, R, E):
    NZ, NB, G = N // 2, N // 4, N * R
    D, FF, W, HH = 256, 512, 4 * R, HEADS // 2 * R
    dma = lambda *shape: pltpu.SemaphoreType.DMA(shape)
    vm = lambda dtype, *shape: pltpu.VMEM(shape, dtype)
    names = dict(
        gb=vm(BF16, L, N, R, D),
        xs=vm(BF16, L, N, R, D),
        meta=vm(I32, N, 8, 256),
        cot=vm(BF16, R, D),
        wp=vm(BF16, L, D, 4 * D),
        we=vm(BF16, L, D, D),
        wqkv=vm(BF16, L, D, 3 * D),
        wo=vm(BF16, L, D, D),
        wu=vm(BF16, L, D, FF),
        wd=vm(BF16, L, FF, D),
        st1=vm(F32, SYNCS, M * N, 4, 128),
        gain=vm(F32, L, 8, D),
        shift=vm(F32, L, 8, D),
        ggain=vm(F32, L, 8, D),
        gshift=vm(F32, L, 8, D),
        iv=vm(F32, L, 8, D),
        moff=vm(F32, N, 8, D),
        move=vm(F32, 8, D),
        le=vm(BF16, E, 1024),
        re=vm(BF16, 1024, D),
        TT=vm(BF16, R, 2 * E),
        ST=vm(BF16, 256, E),
        efT=vm(BF16, D, E),
        HS=vm(BF16, 64, R),
        hx=vm(BF16, L, 64, D),
        A=vm(BF16, R, 64),
        bias=vm(F32, R, G),
        xf=vm(F32, L + 1, R, D),
        xe=vm(BF16, L, 256, D),
        xeT=vm(BF16, D, 256),
        gate=vm(F32, L, E, D),
        bs=vm(BF16, L, E, D),
        num=vm(F32, L, R, D),
        den=vm(F32, L, R, D),
        z0=vm(F32, L, R, D),
        z1=vm(F32, L, R, D),
        z2=vm(F32, L, R, D),
        wkvT=vm(BF16, L, 2 * D, D),
        kvT=vm(BF16, L, 2 * D, G),
        odT=vm(F32, NB, D, R),
        ldT=vm(F32, NB, D, R),
        md=vm(F32, NB, R, D),
        rb=vm(F32, L, NB, R, D),
        pst=vm(BF16, L, HEADS * R, G),
        oraw=vm(F32, L, R, D),
        ob=vm(BF16, L, R, D),
        mb=vm(BF16, L, R, D),
        u=vm(F32, L, R, FF),
        g=vm(BF16, L, R, FF),
        dy=vm(F32, R, D),
        dmix=vm(F32, R, D),
        gy0=vm(F32, R, D),
        local=vm(F32, R, D),
        dxo=vm(F32, R, D),
        dob=vm(F32, R, D),
        dqT=vm(F32, D, R),
        qm=vm(BF16, L, 2, HH, 128),
        q=vm(BF16, L, R, D),
        qT=vm(BF16, D, R),
        dosT=vm(BF16, 128, R),
        dom=vm(BF16, HH, 256),
        sc=vm(F32, 2, max(2 * R, E), W),
        tp=vm(F32, HEADS // 2, R, 128),
        dss=vm(BF16, HH, W),
        dkv=vm(BF16, 2 * D, W),
        gkv=vm(F32, 2 * D, D),
        gg=vm(BF16, 2 * E, 2 * D),
        dn=vm(BF16, 512, 2 * D),
        dproj=vm(BF16, 256, 4 * D),
        dxs=vm(BF16, L, NZ, 2, R, D),
        rs1=vm(BF16, L, NZ, R, D),
        cs=vm(BF16, L, NZ, R, D),
        rs2=vm(BF16, L, NZ, R, D),
        ro=vm(BF16, L, 3, R, D),
        hs=vm(BF16, L, 2, 32, D),
        hr=vm(BF16, L, 2, 32, D),
    )
    names.update(
        gs_early=vm(BF16, L, 2560, 128),
        gs_conv=vm(BF16, L, 2560, 128),
        gs_qkv=vm(BF16, L, 1536, 128),
    )
    sizes = axis_sizes(N, M)
    for g, (_, _, _, rows, stages) in enumerate(GROUPS):
        names[f"go{g}"] = vm(BF16, rows, 128)
        left = rows
        for k, axis in enumerate(stages):
            left //= sizes[axis]
            names[f"ga{g}_{k}"] = vm(BF16, sizes[axis] - 1, left, 128)
            if k < len(stages) - 1:
                names[f"gh{g}_{k}"] = vm(BF16, left, 128)
    names.update(
        ar_s=dma(len(GROUPS)),
        ar_r=dma(sum(2 * len(stages) for *_, stages in GROUPS)),
        ar_l=dma(len(GROUPS)),
        load=dma(9),
        store=dma(2),
        meta_s=dma(1),
        meta_r=dma(1),
        st_s=dma(1),
        st_r=dma(SYNCS),
        ag_s=dma(1),
        agn_r=dma(L),
        agc_r=dma(L, NZ),
        agp_r=dma(L),
        rs_s=dma(1),
        rsp_r=dma(L, NB, 2),
        ro_r=dma(L),
        rsc_r=dma(L),
        hx_s=dma(1),
        hx_r=dma(L),
        hal_s=dma(1),
        hal_r=dma(L),
    )
    return names


IN_NAMES = (
    "x_in", "ids", "edge_src", "edge_dst", "halo", "ef_h", "wp_h", "we_h", "wqkv_h", "wo_h", "wu_h", "wd_h",
    "gain_in", "shift_in", "cot_h",
)
OUT_NAMES = ("out_act", "grad_in", *(f"gout{g}" for g in range(len(GROUPS))), "ggain_out", "gshift_out")


def kernel(N, M, L, names, *args):
    r_ = Refs()
    for name, ref in zip(IN_NAMES + OUT_NAMES + tuple(names), args, strict=True):
        setattr(r_, name, ref)
    R, D = r_.x_in.shape
    E = r_.ef_h.shape[0]
    NZ, NB, G, W = N // 2, N // 4, N * R, 4 * R
    HK = HEADS // 2
    total = float(N * M * R)
    scale = HEAD_DIM ** -0.5
    me = lax.axis_index("nodes")
    rep = lax.axis_index("rep")
    z = me // 2
    par = me % 2
    partner = 2 * z + (1 - par)
    prev = (me + N - 1) % N
    nxt = (me + 1) % N
    zh, zl = z // 2, z % 2
    z_to = lambda t: 2 * ((zh + t // 2) % NB) + (zl + t % 2) % 2
    z_from = lambda t: 2 * ((zh + NB - t // 2) % NB) + (zl + t % 2) % 2

    def remote(src, dst, s_sem, r_sem, **where):
        return pltpu.make_async_remote_copy(
            src_ref=src, dst_ref=dst, send_sem=s_sem, recv_sem=r_sem,
            device_id=where, device_id_type=MESH,
        )

    def send(src, dst, s_sem, r_sem, **where):
        remote(src, dst, s_sem, r_sem, **where).start()

    def send_rows(src, dst, rows, s_sem, r_sem, **where):
        pieces = next(p for p in range(1, rows) if rows % (16 * p) == 0 and rows // p <= 128)
        for at in range(0, rows, rows // pieces):
            cut = pl.ds(at, rows // pieces)
            send(src.at[cut], dst.at[cut], s_sem, r_sem, **where)

    def arrive(dst, r_sem):
        remote(dst, dst, r_sem, r_sem, nodes=partner).wait_recv()

    def sent(src, s_sem):
        remote(src, src, s_sem, s_sem, nodes=partner).wait_send()

    def when(condition, *acts):
        if condition:
            for act in acts:
                act()

    loads = [pltpu.make_async_copy(r_.ef_h, r_.le.at[:, D : 2 * D], r_.load.at[0])] + [
        pltpu.make_async_copy(getattr(r_, f"{name}_h"), getattr(r_, name), r_.load.at[1 + i])
        for i, name in enumerate(("we", "wqkv", "wp", "wo", "wu", "wd", "cot"))
    ]
    own_rows = pltpu.make_async_copy(r_.x_in, r_.gb.at[0, me], r_.load.at[8])
    own_rows.start()
    for load in loads:
        load.start()

    barrier = pltpu.get_barrier_semaphore()
    for dr in range(M):
        for d in range(N):
            if dr + d > 0:
                pl.semaphore_signal(barrier, inc=1, device_id={"rep": (rep + dr) % M, "nodes": (me + d) % N},
                                    device_id_type=MESH)
    pl.semaphore_wait(barrier, M * N - 1)

    def gather_start(l):
        mine = r_.gb.at[l, me]
        for t in range(2, NZ):
            send_rows(mine, mine, R, r_.ag_s.at[0], r_.agc_r.at[l, t], nodes=2 * z_to(t) + par)
        send_rows(mine, mine, R, r_.ag_s.at[0], r_.agn_r.at[l], nodes=partner)
        send_rows(mine, mine, R, r_.ag_s.at[0], r_.agn_r.at[l], nodes=2 * z_to(1) + par)
        send_rows(mine, mine, R, r_.ag_s.at[0], r_.agn_r.at[l], nodes=2 * z_to(1) + 1 - par)

    def gather_pass(l, t):
        piece = r_.gb.at[l, 2 * z_from(t) + par]
        arrive(piece, r_.agc_r.at[l, t])
        send_rows(piece, piece, R, r_.ag_s.at[0], r_.agp_r.at[l], nodes=partner)

    def gather_near(l):
        arrive(r_.gb.at[l, 0:3], r_.agn_r.at[l])

    def gather_far(l):
        arrive(r_.gb.at[l, 0 : NZ - 2], r_.agp_r.at[l])

    def sync_start(k, first, second):
        mine = rep * N + me
        r_.st1[k, mine] = pack(first, second)
        for dr in range(M):
            for d in range(N):
                if dr + d > 0:
                    send(r_.st1.at[k, mine], r_.st1.at[k, mine], r_.st_s.at[0], r_.st_r.at[k],
                         rep=(rep + dr) % M, nodes=(me + d) % N)

    def sync_wait(k):
        arrive(r_.st1.at[k, 0 : M * N - 1], r_.st_r.at[k])

    def sync_moments(k):
        sync_wait(k)
        return unpack(combine_moments(r_.st1[k], float(R)))

    def sync_sums(k):
        sync_wait(k)
        return unpack(jnp.sum(r_.st1[k], 0))

    sizes = axis_sizes(N, M)
    core, row = rep % 2, rep // 2
    places = dict(
        core=(core, lambda t: dict(rep=2 * row + t)),
        y=(row, lambda t: dict(rep=2 * t + core)),
        x=(par, lambda t: dict(nodes=2 * z + t)),
        z=(z, lambda t: dict(nodes=2 * t + par)),
        rep=(rep, lambda t: dict(rep=t)),
        nodes=(me, lambda t: dict(nodes=t)),
    )

    def reduce_step(g, step):
        name, layer, first, rows, stages = GROUPS[g]
        K = len(stages)
        base = sum(2 * len(before) for *_, before in GROUPS[:g])
        gs, out = getattr(r_, f"gs_{name}").at[layer, first : first + rows], getattr(r_, f"go{g}")
        count, offset = [rows], [0]
        for axis in stages:
            count.append(count[-1] // sizes[axis])
            offset.append(offset[-1] + places[axis][0] * count[-1])
        take = lambda start, size: pl.ds(pl.multiple_of(start, 16), size)
        if 1 <= step <= K:
            k = step - 1
            got = getattr(r_, f"ga{g}_{k}")
            arrive(got, r_.ar_r.at[base + k])
            held = gs if k == 0 else getattr(r_, f"gh{g}_{k - 1}")
            index = places[stages[k]][0]
            acc = held[take(index * count[k + 1], count[k + 1])].astype(F32)
            for slot in range(sizes[stages[k]] - 1):
                acc = acc + got[slot].astype(F32)
            if step < K:
                getattr(r_, f"gh{g}_{k}")[...] = acc.astype(BF16)
            else:
                out[take(offset[K], count[K])] = acc.astype(BF16)
        elif step > K:
            k = 2 * K - step
            arrive(out.at[0 : (sizes[stages[k]] - 1) * count[k + 1]], r_.ar_r.at[base + step - 1])
        if step < K:
            held = gs if step == 0 else getattr(r_, f"gh{g}_{step - 1}")
            index, device = places[stages[step]]
            size = sizes[stages[step]]
            for d in range(1, size):
                to = (index + d) % size
                send_rows(held.at[take(to * count[step + 1], count[step + 1])], getattr(r_, f"ga{g}_{step}").at[d - 1],
                     count[step + 1], r_.ar_s.at[g], r_.ar_r.at[base + step], **device(to))
        elif step < 2 * K:
            k = 2 * K - 1 - step
            index, device = places[stages[k]]
            size = sizes[stages[k]]
            here = out.at[take(offset[k + 1], count[k + 1])]
            for d in range(1, size):
                send_rows(here, here, count[k + 1], r_.ar_s.at[g], r_.ar_r.at[base + step],
                          **device((index + d) % size))
        else:
            pltpu.make_async_copy(out, getattr(r_, f"gout{g}"), r_.ar_l.at[g]).start()

    def reduce_drain(g):
        name, _, _, rows, _ = GROUPS[g]
        sent(getattr(r_, f"gs_{name}").at[:, 0 : rows - rows // (M * N)], r_.ar_s.at[g])
        pltpu.make_async_copy(getattr(r_, f"go{g}"), getattr(r_, f"gout{g}"), r_.ar_l.at[g]).wait()

    def put(buf, l, at, value):
        rows = value.shape[0]
        for c in range(value.shape[1] // 128):
            buf[l, at : at + rows] = value[:, 128 * c : 128 * (c + 1)].astype(BF16)
            at += rows
        return at

    lane_head = lax.broadcasted_iota(I32, (R, 128), 1) // HEAD_DIM

    def by_head(parts):
        out = parts[0]
        for k in range(1, HK):
            out = jnp.where(lane_head == k, parts[k], out)
        return out

    r_.meta[me] = jnp.full((8, 256), -1, I32)
    r_.meta[me, 0:1, 0:R] = r_.ids[...].reshape(1, R)
    r_.meta[me, 1:2, 0:48] = r_.halo[...].reshape(1, 48)
    for d in range(1, N):
        send(r_.meta.at[me], r_.meta.at[me], r_.meta_s.at[0], r_.meta_r.at[0], nodes=(me + d) % N)
    own_rows.wait()
    gather_start(0)

    src_row = r_.edge_src[...].reshape(1, E)
    src_row = jnp.where(src_row < R + 24, src_row, src_row + 8)
    dst_row = r_.edge_dst[...].reshape(1, E)
    src_col = jnp.broadcast_to(src_row, (128, E)).T[:, 0:1]
    dst_col = jnp.broadcast_to(dst_row, (128, E)).T[:, 0:1]
    as_mask = lambda cond: cond.astype(F32).astype(BF16)
    r_.le[:, 0:256] = as_mask(src_col == lax.broadcasted_iota(I32, (E, 256), 1))
    target = as_mask(dst_col == lax.broadcasted_iota(I32, (E, 256), 1))
    r_.le[:, 512:768] = target
    r_.le[:, 768:1024] = target
    target = as_mask(dst_row == lax.broadcasted_iota(I32, (R, E), 0))
    r_.TT[:, 0:E] = target
    r_.TT[:, E:] = target
    r_.ST[...] = as_mask(src_row == lax.broadcasted_iota(I32, (256, E), 0))
    r_.dn[R:256] = jnp.zeros((256 - R, 2 * D), BF16)
    r_.dn[256 + R : 512] = jnp.zeros((256 - R, 2 * D), BF16)
    r_.dproj[R:256, 0:D] = jnp.zeros((256 - R, D), BF16)
    r_.dproj[R:256, 2 * D : 3 * D] = jnp.zeros((256 - R, D), BF16)
    halo_col = jnp.broadcast_to(r_.meta[me][1:2, 0:128], (128, 128)).T
    hot = (halo_col[0:48, 0:1] == lax.broadcasted_iota(I32, (48, R), 1)).astype(F32)
    pad = jnp.zeros((8, R), F32)
    r_.HS[...] = jnp.concatenate([hot[0:24], pad, hot[24:48], pad], 0).astype(BF16)
    loads[0].wait()
    r_.efT[...] = r_.le[:, D : 2 * D].T
    for l in range(L):
        for k in range(3):
            r_.gain[l, k : k + 1] = r_.gain_in[k, l : l + 1]
            r_.shift[l, k : k + 1] = r_.shift_in[k, l : l + 1]
    r_.xf[0] = r_.gb[0, me].astype(F32)
    r_.moff[...] = jnp.zeros((N, 8, D), F32)
    r_.move[0:1] = jnp.ones((1, D), F32)
    r_.move[1:2] = jnp.zeros((1, D), F32)
    for load in loads[1:]:
        load.wait()
    for l in range(L):
        r_.wkvT[l] = r_.wqkv[l, :, D:].T

    arrive(r_.meta.at[0 : N - 1], r_.meta_r.at[0])
    id_col = jnp.broadcast_to(r_.meta[me][0:1, 0:R], (128, R)).T[:, 0:1]
    id_row = jnp.concatenate(
        [r_.meta[4 * ((zh + NB - j // 4) % NB) + j % 4][0:1, 0:R] for j in range(N)], 1
    )
    r_.bias[...] = jnp.where(id_col == id_row, 0.0, NEG)

    r_.A[...] = as_mask(r_.meta[me][1:2, 0:64] == lax.broadcasted_iota(I32, (R, 64), 0))

    factor_exp = scale * math.log2(math.e)

    def prepare_queries(l):
        q = dot(r_.xs[l, me], r_.wqkv[l, :, :D]).astype(BF16)
        r_.q[l] = q
        q = q.astype(F32)
        for hf in range(2):
            for k in range(HK):
                part = jnp.where(lane_head == k, q[:, 128 * hf : 128 * (hf + 1)], 0.0)
                r_.qm[l, hf, k * R : (k + 1) * R] = part.astype(BF16)

    def head_dims(hf, k, base=0):
        first = base + hf * 128 + k * HEAD_DIM
        return slice(first, first + HEAD_DIM)

    def head_rows(hf, k, count=1):
        return slice((hf * HK + k) * R, (hf * HK + k + count) * R)

    def lane_half(hf):
        return slice(hf * 128, (hf + 1) * 128)

    def half_of(i):
        return (zh + NB - i) % NB, slice(i * W, (i + 1) * W)

    def attention_keys(l, i):
        half, rows = half_of(i)
        x = r_.xs[l, pl.ds(4 * half, 4)].reshape(W, D)
        r_.kvT[l, :, rows] = dot_nt(r_.wkvT[l], x).astype(BF16)

    def attention_heads(l, i, hfs):
        _, rows = half_of(i)
        for hf in hfs:
            lanes = lane_half(hf)
            ones = jnp.ones((HEAD_DIM, W), BF16)
            for c in range(HK // 2):
                r_.sc[c % 2, 0 : 2 * R] = dot(r_.qm[l, hf, 2 * c * R : 2 * (c + 1) * R], r_.kvT[l, lanes, rows])
                for k in range(2):
                    for at in range(0, R, STRIP):
                        s = r_.sc[c % 2, k * R + at : k * R + at + STRIP] + r_.bias[at : at + STRIP, rows]
                        top = jnp.max(s, 1, keepdims=True)
                        e = jnp.exp2((s - top) * factor_exp)
                        r_.tp[2 * c + k, at : at + STRIP] = jnp.broadcast_to(top, (STRIP, 128))
                        first = (hf * HK + 2 * c + k) * R + at
                        r_.pst[l, first : first + STRIP, rows] = e.astype(BF16)
                for k in range(2):
                    h = 2 * c + k
                    left = jnp.concatenate([r_.kvT[l, head_dims(hf, h, D), rows], ones], 0)
                    o = dot_nt(left, r_.pst[l, head_rows(hf, h), rows])
                    r_.odT[i, head_dims(hf, h)] = o[0:HEAD_DIM]
                    r_.ldT[i, head_dims(hf, h)] = o[HEAD_DIM:]
            r_.md[i, :, lanes] = by_head([r_.tp[k] for k in range(HK)])

    def attention_end(l):
        tops = [r_.md[i].T for i in range(NB)]
        top = tops[0]
        for i in range(1, NB):
            top = jnp.maximum(top, tops[i])
        factors = [jnp.exp2((tops[i] - top) * factor_exp) for i in range(NB)]
        inv = 1.0 / sum(factors[i] * r_.ldT[i] for i in range(NB))
        o = jnp.zeros((D, R), F32)
        for i in range(NB):
            r_.rb[l, i] = (factors[i] * inv).T
            o = o + factors[i] * inv * r_.odT[i]
        o = o.T
        r_.oraw[l] = o
        ob = o.astype(BF16)
        r_.ob[l] = ob
        t1 = r_.xf[l] + dot(ob, r_.wo[l])
        r_.z1[l] = t1
        mean1 = col_sum(t1) / R
        return mean1, col_sum((t1 - mean1) * (t1 - mean1))

    def convolution(l):
        xs = r_.xs
        xb = xs[l, me]
        r_.xe[l, 0:R] = xb
        arrive(r_.xe.at[l, R : R + 64], r_.hx_r.at[l])
        xe = r_.xe[l]
        made = dot(xe, r_.wp[l])
        pd_high, pd_low = split(made[:, 2 * D : 3 * D])
        r_.re[0:256] = made[:, 3 * D :].astype(BF16)
        r_.re[256:512] = r_.we[l]
        r_.re[512:768] = pd_high
        r_.re[768:1024] = pd_low
        r_.gate[l] = dot(r_.le[...], r_.re[...])
        r_.bs[l] = dot(r_.le[:, 0:256], made[:, D : 2 * D].astype(BF16)).astype(BF16)
        for at in range(0, E, 64):
            here = slice(at, at + 64)
            gate = sigmoid(r_.gate[l, here])
            r_.gate[l, here] = gate
            high, low = split(jnp.concatenate([gate * r_.bs[l, here].astype(F32), gate], 1))
            r_.gg[here] = high
            r_.gg[E + at : E + at + 64] = low
        num_den = dot(r_.TT[...], r_.gg[...])
        pa, num, den = made[0:R, 0:D], num_den[:, 0:D], num_den[:, D:]
        r_.num[l] = num
        r_.den[l] = den
        msg = pa + num / (den + GATE_EPS)
        r_.z0[l] = msg
        mean0 = col_sum(msg) / R
        return mean0, col_sum((msg - mean0) * (msg - mean0))

    def forward(l):
        def ready(js):
            for j in js:
                moved = (r_.gb[l, j].astype(F32) + r_.moff[j, 0:1]) * r_.move[0:1] + r_.move[1:2]
                r_.xs[l, j] = moved.astype(BF16)

        r_.xs[l, me] = r_.xf[l].astype(BF16)
        r_.hx[l] = dot(r_.HS[...], r_.xs[l, me]).astype(BF16)
        send(r_.hx.at[l, 0:32], r_.xe.at[l, R + 32 : R + 64], r_.hx_s.at[0], r_.hx_r.at[l], nodes=prev)
        send(r_.hx.at[l, 32:64], r_.xe.at[l, R : R + 32], r_.hx_s.at[0], r_.hx_r.at[l], nodes=nxt)
        prepare_queries(l)
        for t in range(2, NZ):
            gather_pass(l, t)
        mean0, sq0 = convolution(l)
        sync_start(3 * l, mean0, sq0)
        gather_near(l)
        ready([partner, 2 * z_from(1) + par, 2 * z_from(1) + 1 - par])

        attention_keys(l, 0)
        attention_heads(l, 0, (0, 1))
        gather_far(l)
        ready([2 * z_from(t) + p for t in range(2, NZ) for p in range(2)])
        for i in range(1, NB):
            attention_keys(l, i)
            attention_heads(l, i, (0, 1))
        mean1, sq1 = attention_end(l)
        sync_start(3 * l + 1, mean1, sq1)
        mean0, sq0 = sync_moments(3 * l)
        inv0 = lax.rsqrt(sq0 / total + NORM_EPS)
        r_.iv[l, 0:1] = inv0
        z0 = (r_.z0[l] - mean0) * inv0
        r_.z0[l] = z0
        n0 = z0 * r_.gain[l, 0:1] + r_.shift[l, 0:1]
        r_.local[...] = r_.xf[l] + n0 * sigmoid(n0)
        mean1, sq1 = sync_moments(3 * l + 1)
        inv1 = lax.rsqrt(sq1 / total + NORM_EPS)
        r_.iv[l, 1:2] = inv1
        z1 = (r_.z1[l] - mean1) * inv1
        r_.z1[l] = z1
        mix = r_.local[...] + z1 * r_.gain[l, 1:2] + r_.shift[l, 1:2]
        mb = mix.astype(BF16)
        r_.mb[l] = mb
        u = dot(mb, r_.wu[l])
        r_.u[l] = u
        g = (u * sigmoid(u)).astype(BF16)
        r_.g[l] = g
        y = mix + dot(g, r_.wd[l])
        r_.z2[l] = y
        mean = col_sum(y) / R
        cent = y - mean
        k = 3 * l + 2
        sync_start(k, mean, col_sum(cent * cent))

        if l < L - 1:
            r_.gb[l + 1, me] = cent.astype(BF16)
            gather_start(l + 1)

        if l == L - 1:
            dy = r_.cot[...].astype(F32)
            sync_start(3 * L, col_sum(dy), col_sum(dy * cent))

        tot_mean, tot_sq = sync_moments(k)
        inv2 = lax.rsqrt(tot_sq / total + NORM_EPS)
        r_.iv[l, 2:3] = inv2
        z2 = (r_.z2[l] - tot_mean) * inv2
        r_.z2[l] = z2
        gain, shift = r_.gain[l, 2:3], r_.shift[l, 2:3]
        r_.xf[l + 1] = z2 * gain + shift

        if l == L - 1:
            sync_wait(3 * L)
            sums, means = r_.st1[3 * L], r_.st1[k][:, 0:2]
            mean = jnp.mean(means, 0)
            dy_sum = jnp.sum(sums[:, 0:2], 0)
            dy_cent = jnp.sum(sums[:, 2:4] + (means - mean) * sums[:, 0:2], 0)
            dy_sum, dy_cent = unpack(jnp.concatenate([dy_sum, dy_cent], 0))
            r_.gshift[l, 2:3] = dy_sum
            r_.ggain[l, 2:3] = dy_cent * inv2

        for j in range(N):
            tile = r_.st1[k, rep * N + j]
            r_.moff[j, 0:1] = jnp.concatenate([tile[0:1], tile[1:2]], 1) - tot_mean
        r_.move[0:1] = inv2 * gain
        r_.move[1:2] = shift

    for l in range(L):
        forward(l)
    act_copy = pltpu.make_async_copy(r_.xf.at[L], r_.out_act, r_.store.at[0])
    act_copy.start()

    def back_feed_forward(l, k):
        s2, g2 = r_.gshift[l, 2:3], r_.ggain[l, 2:3]
        d3 = r_.gain[l, 2:3] * r_.iv[l, 2:3] * (r_.dy[...] - s2 / total - r_.z2[l] * (g2 / total))
        db = d3.astype(BF16)
        dub = (dot_nt(db, r_.wd[l]) * silu_slope(r_.u[l])).astype(BF16)
        dmix = d3 + dot_nt(dub, r_.wu[l])
        r_.dmix[...] = dmix
        n0 = r_.z0[l] * r_.gain[l, 0:1] + r_.shift[l, 0:1]
        gy0 = dmix * silu_slope(n0)
        sync_start(k, col_sum(dmix), col_sum(dmix * r_.z1[l]))
        sync_start(k + 1, col_sum(gy0), col_sum(gy0 * r_.z0[l]))
        r_.gy0[...] = gy0
        at = put(r_.gs_early, l, 512, dot_tn(r_.mb[l], dub))
        put(r_.gs_early, l, at, dot_tn(r_.g[l], db))
        r_.xeT[...] = r_.xe[l].T
        r_.qT[...] = r_.q[l].T

    def back_norms(l, k):
        s1, g1 = sync_sums(k)
        r_.gshift[l, 1:2] = s1
        r_.ggain[l, 1:2] = g1
        dmix = r_.dmix[...]
        d2 = r_.gain[l, 1:2] * r_.iv[l, 1:2] * (dmix - s1 / total - r_.z1[l] * (g1 / total))
        dab = d2.astype(BF16)
        r_.dxo[...] = dmix + d2
        r_.dob[...] = dot_nt(dab, r_.wo[l]).astype(BF16).astype(F32)
        put(r_.gs_early, l, 0, dot_tn(r_.ob[l], dab))
        r_.gkv[...] = jnp.zeros((2 * D, D), F32)
        r_.dqT[...] = jnp.zeros((D, R), F32)

    def back_half(i):
        t1 = (i + 1) % NB
        half = (zh + t1) % NB
        place = (NB - t1) % NB
        return place, half, slice(place * W, (place + 1) * W)

    def back_heads(l, i, hf):
        place, half, rows = back_half(i)
        if True:
            lanes = lane_half(hf)
            dos = r_.dob[:, lanes] * r_.rb[l, place, :, lanes]
            prod = dos * r_.oraw[l, :, lanes]
            for k in range(HK):
                r_.dom[k * R : (k + 1) * R, 0:128] = jnp.where(lane_head == k, dos, 0.0).astype(BF16)
                r_.dom[k * R : (k + 1) * R, 128:256] = jnp.where(lane_head == k, -prod, 0.0).astype(BF16)
            r_.dosT[...] = dos.T.astype(BF16)
            values = slice(D + hf * 128, D + (hf + 1) * 128)
            right = jnp.concatenate([r_.kvT[l, values, rows], jnp.ones((128, W), BF16)], 0)
            for c in range(HK // 2):
                both = slice(2 * c * R, 2 * (c + 1) * R)
                r_.sc[c % 2, 0 : 2 * R] = dot(r_.dom[both], right)
                for k in range(2):
                    for at in range(0, R, STRIP):
                        first = (hf * HK + 2 * c + k) * R + at
                        e = r_.pst[l, first : first + STRIP, rows].astype(F32)
                        ds = e * r_.sc[c % 2, k * R + at : k * R + at + STRIP]
                        r_.dss[(2 * c + k) * R + at : (2 * c + k) * R + at + STRIP] = ds.astype(BF16)
                for k in range(2):
                    h = 2 * c + k
                    mine, dims = slice(h * R, (h + 1) * R), head_dims(hf, h)
                    r_.dqT[dims] += dot_nt(r_.kvT[l, dims, rows], r_.dss[mine])
                    r_.dkv[dims] = (dot(r_.qT[dims], r_.dss[mine]) * scale).astype(BF16)
                    dv = dot(r_.dosT[h * HEAD_DIM : (h + 1) * HEAD_DIM], r_.pst[l, head_rows(hf, h), rows])
                    r_.dkv[head_dims(hf, h, D)] = dv.astype(BF16)

    def back_rows(l, i):
        _, half, _ = back_half(i)
        dx = dot(r_.wqkv[l, :, D:], r_.dkv[...]).T
        r_.dxs[l, pl.ds(2 * half, 2)] = dx.astype(BF16).reshape(2, 2, R, D)

        if i < NB - 1:
            for t in (2 * (i + 1), 2 * (i + 1) + 1):
                zb = z_to(t)
                send_rows(r_.dxs.at[l, zb, 1 - par], r_.rs1.at[l, zb], R,
                          r_.rs_s.at[0], r_.rsp_r.at[l, i, t % 2], nodes=partner)

        else:
            near = z_to(1)
            send_rows(r_.dxs.at[l, z, 1 - par], r_.ro.at[l, 0], R, r_.rs_s.at[0], r_.ro_r.at[l], nodes=partner)
            send_rows(r_.dxs.at[l, near, par], r_.ro.at[l, 1], R, r_.rs_s.at[0], r_.ro_r.at[l], nodes=2 * near + par)
            send_rows(r_.dxs.at[l, near, 1 - par], r_.ro.at[l, 2], R, r_.rs_s.at[0], r_.ro_r.at[l],
                 nodes=2 * near + 1 - par)

        r_.gkv[...] += dot(r_.dkv[...], r_.xs[l, pl.ds(4 * half, 4)].reshape(W, D))

    def pass_on(l, i, t):
        zb = z_to(t)
        arrive(r_.rs1.at[l, zb], r_.rsp_r.at[l, i, t % 2])
        both = r_.dxs[l, zb, par].astype(F32) + r_.rs1[l, zb].astype(F32)
        r_.cs[l, zb] = both.astype(BF16)
        send_rows(r_.cs.at[l, zb], r_.rs2.at[l, z], R, r_.rs_s.at[0], r_.rsc_r.at[l], nodes=2 * zb + par)

    def back_convolution(l, k):
        s0, g0 = unpack(jnp.sum(r_.st1[k + 1], 0))
        r_.gshift[l, 0:1] = s0
        r_.ggain[l, 0:1] = g0
        inv_den = 1.0 / (r_.den[l] + GATE_EPS)
        dm = r_.gain[l, 0:1] * r_.iv[l, 0:1] * (r_.gy0[...] - s0 / total - r_.z0[l] * (g0 / total))
        dnum = dm * inv_den
        dden = -dnum * r_.num[l] * inv_den
        high, low = split(jnp.concatenate([dnum, dden], 1))
        r_.dn[0:R] = high
        r_.dn[256 : 256 + R] = low
        r_.sc[0, 0:E, 0 : 2 * D] = dot(r_.le[:, 512:1024], r_.dn[...])
        for at in range(0, E, 64):
            here = slice(at, at + 64)
            gate, dnum_e = r_.gate[l, here], r_.sc[0, here, 0:D]
            dgp = (dnum_e * r_.bs[l, here].astype(F32) + r_.sc[0, here, D : 2 * D]) * gate * (1.0 - gate)
            r_.gg[here, 0:D] = (dnum_e * gate).astype(BF16)
            r_.gg[here, D:] = dgp.astype(BF16)
        ext = dot(r_.ST[...], r_.gg[0:E]).astype(BF16)
        r_.dproj[0:R, 0:D] = dm.astype(BF16)
        r_.dproj[:, D : 2 * D] = ext[:, 0:D]
        r_.dproj[0:R, 2 * D : 3 * D] = dot(r_.TT[:, 0:E], r_.gg[0:E, D:]).astype(BF16)
        r_.dproj[:, 3 * D :] = ext[:, D:]
        dxe = dot_nt(r_.dproj[...], r_.wp[l])
        r_.hs[l, 0] = dxe[R : R + 32].astype(BF16)
        r_.hs[l, 1] = dxe[R + 32 : R + 64].astype(BF16)
        r_.dxo[...] += dxe[0:R]

    def send_halo(l):
        send(r_.hs.at[l, 0], r_.hr.at[l, 1], r_.hal_s.at[0], r_.hal_r.at[l], nodes=prev)
        send(r_.hs.at[l, 1], r_.hr.at[l, 0], r_.hal_s.at[0], r_.hal_r.at[l], nodes=nxt)

    def conv_weight_grads(l):
        at = put(r_.gs_conv, l, 0, dot(r_.xeT[...], r_.dproj[...]))
        put(r_.gs_conv, l, at, dot(r_.efT[...], r_.gg[0:E, D:]))

    def back_input(l):
        dx = r_.dxo[...]
        dx = dx + r_.dxs[l, z, par].astype(F32)
        arrive(r_.ro.at[l], r_.ro_r.at[l])
        for slot in range(3):
            dx = dx + r_.ro[l, slot].astype(F32)
        if NZ > 2:
            arrive(r_.rs2.at[l, 0 : NZ - 2], r_.rsc_r.at[l])
        for t in range(2, NZ):
            dx = dx + r_.rs2[l, z_from(t)].astype(F32)
        arrive(r_.hr.at[l], r_.hal_r.at[l])
        back = jnp.concatenate(
            [r_.hr[l, 0].astype(F32)[0:24], r_.hr[l, 1].astype(F32)[0:24], jnp.zeros((16, D), F32)], 0
        )
        return dx + dot(r_.A[...], back.astype(BF16))

    r_.dy[...] = r_.cot[...].astype(F32)

    E1, C1, Q1, E0, C0, QK0, V0 = range(len(GROUPS))

    def steps(*pairs):
        return [functools.partial(reduce_step, g, k) for g, k in pairs]

    r_.dy[...] = r_.cot[...].astype(F32)

    def backward(b):
        l = L - 1 - b
        first, last = b == 0, b == L - 1
        k = 3 * L + 1 + 2 * b
        back_feed_forward(l, k)
        when(last, *steps((E1, 3), (Q1, 2)))
        back_norms(l, k)
        if first:
            when(True, *steps((E1, 0)))
            back_heads(l, 0, 0)
            back_heads(l, 0, 1)
            back_rows(l, 0)
            when(True, *steps((E1, 1)))
            sync_wait(k + 1)
            back_convolution(l, k)
            send_halo(l)
            pass_on(l, 0, 2)
            back_heads(l, 1, 0)
            pass_on(l, 0, 3)
            back_heads(l, 1, 1)
            back_rows(l, 1)
            conv_weight_grads(l)
            when(True, *steps((C1, 0)))
        else:
            when(True, *steps((C1, 3), (E1, 4), (E0, 0)))
            sync_wait(k + 1)
            back_convolution(l, k)
            back_heads(l, 0, 0)
            send_halo(l)
            when(True, *steps((Q1, 3), (E1, 5), (C1, 4), (E0, 1)))
            conv_weight_grads(l)
            back_heads(l, 0, 1)
            back_rows(l, 0)
            when(True, *steps((C0, 0), (E0, 2), (Q1, 4), (E1, 6), (C1, 5)))
            back_heads(l, 1, 0)
            when(True, *steps((C0, 1), (E0, 3), (Q1, 5), (C1, 6)))
            for t in range(2, NZ):
                pass_on(l, 0, t)
            back_heads(l, 1, 1)
            back_rows(l, 1)
            when(True, *steps((C0, 2), (E0, 4), (Q1, 6)))
        dqb = (r_.dqT[...].T * scale).astype(BF16)
        r_.dxo[...] += dot_nt(dqb, r_.wqkv[l, :, 0:D])
        at = put(r_.gs_qkv, l, 0, dot(r_.xeT[:, 0:R], dqb))
        put(r_.gs_qkv, l, at, r_.gkv[...].T)
        if first:
            when(True, *steps((Q1, 0), (C1, 1)))
            dx = back_input(l)
            r_.dy[...] = dx
            below = L - 2
            sync_start(SYNCS - 1, col_sum(dx), col_sum(dx * r_.z2[below]))
            when(True, *steps((E1, 2), (Q1, 1)))
            s2, g2 = sync_sums(SYNCS - 1)
            r_.gshift[below, 2:3] = s2
            r_.ggain[below, 2:3] = g2
            when(True, *steps((C1, 2)))

    for b in range(L):
        backward(b)
    for step in steps((QK0, 0), (V0, 0), (E0, 5), (C0, 3), (V0, 1), (QK0, 1)):
        step()
    r_.dy[...] = back_input(0)
    in_copy = pltpu.make_async_copy(r_.dy, r_.grad_in, r_.store.at[1])
    in_copy.start()
    for step in steps(
        (E0, 6), (C0, 4), (V0, 2), (QK0, 2),
        (E0, 7), (C0, 5), (V0, 3), (QK0, 3),
        (E0, 8), (C0, 6), (V0, 4), (QK0, 4),
    ):
        step()
    for l in range(L):
        for k in range(3):
            r_.ggain_out[k, l : l + 1] = r_.ggain[l, k : k + 1]
            r_.gshift_out[k, l : l + 1] = r_.gshift[l, k : k + 1]
    for g in range(len(GROUPS)):
        reduce_drain(g)
    sent(r_.meta.at[0 : N - 1], r_.meta_s.at[0])
    sent(r_.st1.at[:, 0 : M * N - 1], r_.st_s.at[0])
    sent(r_.gb.at[:, 0 : 3 + 2 * (NZ - 2)], r_.ag_s.at[0])
    sent(r_.gb.at[:, 0 : 2 * (NB - 1) + 3 + NZ - 2], r_.rs_s.at[0])
    sent(r_.hs, r_.hal_s.at[0])
    sent(r_.hx, r_.hx_s.at[0])
    act_copy.wait()
    in_copy.wait()


def finish_kernel(act_h, gin_h, *refs):
    n = len(GROUPS)
    held, (ggain_h, gshift_h), refs = refs[:n], refs[n : n + 2], refs[n + 2 :]
    act_o, gin_o, proj_o, edge_o, qkv_o, out_o, up_o, down_o, ggain_o, gshift_o = refs[:10]
    summed, refs = refs[10 : 10 + n], refs[10 + n :]
    act, gin, proj, edge, qkv, out, up, down, in_sem, out_sem = refs
    loads = [
        pltpu.make_async_copy(src, dst, in_sem.at[i])
        for i, (src, dst) in enumerate(zip(held + (act_h, gin_h), summed + (act, gin), strict=True))
    ]
    for load in loads:
        load.start()
    ggain_o[...] = ggain_h[...]
    gshift_o[...] = gshift_h[...]
    stores = []

    def store(src, dst):
        copy = pltpu.make_async_copy(src, dst, out_sem.at[len(stores)])
        copy.start()
        stores.append(copy)

    def widen(dst, l, g, at, first=0, last=None):
        rows = dst.shape[1]
        for c in range(first, dst.shape[2] // 128 if last is None else last):
            dst[l, :, 128 * c : 128 * (c + 1)] = summed[g][at : at + rows].astype(F32)
            at += rows
        return at

    for g, (name, l, first, rows, _) in enumerate(GROUPS):
        loads[g].wait()
        if name == "early":
            at = widen(out, l, g, 0)
            store(out.at[l], out_o.at[l])
            at = widen(up, l, g, at)
            store(up.at[l], up_o.at[l])
            widen(down, l, g, at)
            store(down.at[l], down_o.at[l])
        elif name == "conv":
            at = widen(proj, l, g, 0)
            store(proj.at[l], proj_o.at[l])
            widen(edge, l, g, at)
            store(edge.at[l], edge_o.at[l])
        else:
            widen(qkv, l, g, 0, first // 256, (first + rows) // 256)
            if first + rows == 1536:
                store(qkv.at[l], qkv_o.at[l])
    for i, (src, dst) in enumerate(((act, act_o), (gin, gin_o))):
        loads[n + i].wait()
        store(src, dst)
    for copy in stores:
        copy.wait()


def fused_device(
    N, M, node_input, edge_feat, graph_ids, edge_src, edge_dst, halo_send, w_proj, w_edge, w_qkv,
    w_out, w_up, w_down, norm_gain, norm_shift, cotangent,
):
    R, D = node_input.shape
    E = edge_feat.shape[0]
    L = w_proj.shape[0]
    names = scratch_list(N, M, L, R, E)
    vmem = pl.BlockSpec(memory_space=pltpu.VMEM)
    hbm = pl.BlockSpec(memory_space=pltpu.HBM)
    shape = jax.ShapeDtypeStruct
    rows = shape((R, D), F32)
    norm = shape((3, L, D), F32)
    groups = [shape((rows_g, 128), BF16) for _, _, _, rows_g, _ in GROUPS]
    outs = pl.pallas_call(
        functools.partial(kernel, N, M, L, tuple(names)),
        out_shape=[rows, rows, *groups, norm, norm],
        in_specs=[hbm] + [vmem] * 4 + [hbm] * 7 + [vmem] * 2 + [hbm],
        out_specs=[hbm] * (2 + len(GROUPS)) + [vmem] * 2,
        scratch_shapes=list(names.values()),
        compiler_params=pltpu.CompilerParams(
            collective_id=0, has_side_effects=True, vmem_limit_bytes=60 << 20
        ),
        name="layers",
    )(node_input, graph_ids, edge_src, edge_dst, halo_send, edge_feat, w_proj, w_edge, w_qkv, w_out, w_up,
      w_down, norm_gain.transpose(1, 0, 2), norm_shift.transpose(1, 0, 2), cotangent)
    weights = [shape(w.shape, F32) for w in (w_proj, w_edge, w_qkv, w_out, w_up, w_down)]
    results = pl.pallas_call(
        finish_kernel,
        out_shape=[rows, rows, *weights, norm, norm],
        in_specs=[hbm] * (2 + len(GROUPS)) + [vmem] * 2,
        out_specs=[hbm] * 8 + [vmem] * 2,
        scratch_shapes=[pltpu.VMEM(s.shape, s.dtype) for s in (*groups, rows, rows, *weights)]
        + [pltpu.SemaphoreType.DMA((len(GROUPS) + 2,)), pltpu.SemaphoreType.DMA((14,))],
        compiler_params=pltpu.CompilerParams(vmem_limit_bytes=60 << 20),
        name="gradients",
    )(*outs)
    ggain, gshift = results[8].transpose(1, 0, 2), results[9].transpose(1, 0, 2)
    return (*results[:8], ggain, gshift)


BLOCK_CAP = 2048


def extended_2(block, sides, width):
    for axis, dim in sides:
        count = lax.axis_size(axis)
        forward = [(i, i + 1) for i in range(count - 1)]
        forward.append((count - 1, 0))
        backward = [(target, source) for source, target in forward]
        low = lax.ppermute(
            lax.slice_in_dim(block, block.shape[dim] - width, None, axis=dim), axis, forward
        )
        high = lax.ppermute(lax.slice_in_dim(block, 0, width, axis=dim), axis, backward)
        block = jnp.concatenate([low, block, high], axis=dim)
    return block


def block_length(total_rows, upper_limit):
    for length in range(min(total_rows, upper_limit), 0, -1):
        if total_rows % length == 0:
            return length
    return 1


def outer_product(left, right):
    return lax.dot_general(
        left, right, (((0,), (0,)), ((), ())), preferred_element_type=jnp.float32
    )


def times_transposed(left, weight):
    return lax.dot_general(
        left, weight, (((1,), (1,)), ((), ())), preferred_element_type=jnp.float32
    )


def forward_product(left, weight):
    return jnp.dot(left, weight, preferred_element_type=jnp.float32)


def silu_slope_plain(inputs):
    logistic = jax.nn.sigmoid(inputs)
    return logistic * (1.0 + inputs * (1.0 - logistic))


def normalize(inputs, gain_row, shift_row, node_total):
    batch_mean = lax.psum(jnp.sum(inputs, 0), ("nodes", "rep")) / node_total
    centred = inputs - batch_mean
    batch_var = lax.psum(jnp.sum(centred * centred, 0), ("nodes", "rep")) / node_total
    inv_std = lax.rsqrt(batch_var + NORM_EPS)
    standard = (inputs - batch_mean) * inv_std
    return (standard * gain_row + shift_row, standard, inv_std)


def normalize_back(grad_out, standard, inv_std, gain_row, node_total):
    shift_grad, gain_grad = lax.psum(
        (jnp.sum(grad_out, 0), jnp.sum(grad_out * standard, 0)), ("nodes", "rep")
    )
    grad_in = (
        gain_row
        * inv_std
        * (grad_out - shift_grad / node_total - standard * gain_grad / node_total)
    )
    return (grad_in, gain_grad, shift_grad)


def exchange_sources(outgoing):
    halo_rows = outgoing.shape[0] // 2
    grown = extended_2(outgoing, (("nodes", 0),), halo_rows)
    return jnp.concatenate([grown[:halo_rows], grown[3 * halo_rows :]], 0)


def return_sources(incoming_grad):
    halo_rows = incoming_grad.shape[0] // 2
    grown = extended_2(incoming_grad.astype(jnp.bfloat16), (("nodes", 0),), halo_rows).astype(
        incoming_grad.dtype
    )
    return jnp.concatenate([grown[:halo_rows], grown[3 * halo_rows :]], 0)


def attend_forward(query_rows, key_rows, value_rows, local_graphs, group_graphs):
    row_count = query_rows.shape[0]
    score_scale = HEAD_DIM ** (-0.5)
    queries = query_rows.reshape(row_count, HEADS, HEAD_DIM)

    def add_piece(carried, kv_piece, first_row):
        key_piece, value_piece = kv_piece
        piece_rows = key_piece.shape[0]
        block_len = block_length(piece_rows, BLOCK_CAP)

        def add_block(block_state, block_index):
            row_max, row_sum, accumulated = block_state
            block_start = block_index * block_len
            key_block = lax.dynamic_slice_in_dim(key_piece, block_start, block_len, 0).reshape(
                block_len, HEADS, HEAD_DIM
            )
            value_block = lax.dynamic_slice_in_dim(value_piece, block_start, block_len, 0).reshape(
                block_len, HEADS, HEAD_DIM
            )
            key_graphs = lax.dynamic_slice_in_dim(
                group_graphs, first_row + block_start, block_len, 0
            )
            same_graph = (local_graphs[:, None] == key_graphs[None, :])[None]
            scores = (
                jnp.einsum("qhd,khd->hqk", queries, key_block, preferred_element_type=jnp.float32)
                * score_scale
            )
            scores = jnp.where(same_graph, scores, NEG)
            new_max = jnp.maximum(row_max, jnp.max(scores, 2))
            weights = jnp.where(same_graph, jnp.exp(scores - new_max[:, :, None]), 0.0)
            factor = jnp.exp(row_max - new_max)
            row_sum = row_sum * factor + jnp.sum(weights, 2)
            contrib = jnp.einsum(
                "hqk,khd->qhd",
                weights.astype(jnp.bfloat16),
                value_block,
                preferred_element_type=jnp.float32,
            )
            accumulated = accumulated * jnp.transpose(factor)[:, :, None] + contrib
            return ((new_max, row_sum, accumulated), None)

        carried, _ = lax.scan(add_block, carried, jnp.arange(piece_rows // block_len))
        return carried

    start_state = (
        jnp.full((HEADS, row_count), NEG, jnp.float32),
        jnp.zeros((HEADS, row_count), jnp.float32),
        jnp.zeros((row_count, HEADS, HEAD_DIM), jnp.float32),
    )
    row_max, row_sum, accumulated = add_piece(
        start_state,
        (
            lax.all_gather(key_rows, "nodes", axis=0, tiled=True),
            lax.all_gather(value_rows, "nodes", axis=0, tiled=True),
        ),
        jnp.int32(0),
    )
    attn_raw = accumulated / jnp.transpose(row_sum)[:, :, None]
    log_sum = row_max + jnp.log(row_sum)
    return (attn_raw, log_sum)


def attend_backward(
    query_rows, key_rows, value_rows, grad_low, attn_raw, log_sum, local_graphs, group_graphs
):
    row_count = query_rows.shape[0]
    model_width = HEADS * HEAD_DIM
    score_scale = HEAD_DIM ** (-0.5)
    queries = query_rows.reshape(row_count, HEADS, HEAD_DIM)
    grad_heads = grad_low.reshape(row_count, HEADS, HEAD_DIM)
    row_delta = jnp.einsum("qhd,qhd->hq", grad_heads.astype(jnp.float32), attn_raw)

    def score_block(key_block, value_block, key_graphs):
        same_graph = (local_graphs[:, None] == key_graphs[None, :])[None]
        scores = (
            jnp.einsum("qhd,khd->hqk", queries, key_block, preferred_element_type=jnp.float32)
            * score_scale
        )
        attn_weights = jnp.exp(jnp.where(same_graph, scores - log_sum[:, :, None], NEG))
        grad_weights = jnp.einsum(
            "qhd,khd->hqk", grad_heads, value_block, preferred_element_type=jnp.float32
        )
        grad_scores = (attn_weights * (grad_weights - row_delta[:, :, None])).astype(jnp.bfloat16)
        return (attn_weights, grad_scores)

    def key_terms(attn_weights, grad_scores, block_len):
        grad_keys = (
            jnp.einsum("hqk,qhd->khd", grad_scores, queries, preferred_element_type=jnp.float32)
            * score_scale
        )
        grad_values = jnp.einsum(
            "hqk,qhd->khd",
            attn_weights.astype(jnp.bfloat16),
            grad_heads,
            preferred_element_type=jnp.float32,
        )
        return jnp.concatenate(
            [
                grad_keys.reshape(block_len, model_width),
                grad_values.reshape(block_len, model_width),
            ],
            1,
        )

    def query_term(grad_scores, key_block):
        return (
            jnp.einsum("hqk,khd->qhd", grad_scores, key_block, preferred_element_type=jnp.float32)
            * score_scale
        )

    group_rows = group_graphs.shape[0]

    def add_piece(carried, kv_piece, first_row):
        key_piece, value_piece = kv_piece
        piece_rows = key_piece.shape[0]
        block_len = block_length(piece_rows, BLOCK_CAP)

        def add_block(block_state, block_index):
            grad_query, buffer = block_state
            block_start = block_index * block_len
            key_block = lax.dynamic_slice_in_dim(key_piece, block_start, block_len, 0).reshape(
                block_len, HEADS, HEAD_DIM
            )
            value_block = lax.dynamic_slice_in_dim(value_piece, block_start, block_len, 0).reshape(
                block_len, HEADS, HEAD_DIM
            )
            place = first_row + block_start
            key_graphs = lax.dynamic_slice_in_dim(group_graphs, place, block_len, 0)
            attn_weights, grad_scores = score_block(key_block, value_block, key_graphs)
            grad_query = grad_query + query_term(grad_scores, key_block)
            block_terms = key_terms(attn_weights, grad_scores, block_len)
            current = lax.dynamic_slice_in_dim(buffer, place, block_len, 0)
            buffer = lax.dynamic_update_slice_in_dim(buffer, current + block_terms, place, 0)
            return ((grad_query, buffer), None)

        carried, _ = lax.scan(add_block, carried, jnp.arange(piece_rows // block_len))
        return carried

    start_state = (
        jnp.zeros((row_count, HEADS, HEAD_DIM), jnp.float32),
        jnp.zeros((group_rows, 2 * model_width), jnp.float32),
    )
    grad_query, buffer = add_piece(
        start_state,
        (
            lax.all_gather(key_rows, "nodes", axis=0, tiled=True),
            lax.all_gather(value_rows, "nodes", axis=0, tiled=True),
        ),
        jnp.int32(0),
    )
    grad_kv = lax.psum_scatter(buffer, "nodes", scatter_dimension=0, tiled=True)
    return (
        grad_query.reshape(row_count, model_width),
        grad_kv[:, :model_width],
        grad_kv[:, model_width:],
    )


def layer_forward(
    hidden, params, edge_feat, edge_src, edge_dst, halo_send, local_graphs, group_graphs, node_total
):
    w_proj, w_edge, w_qkv, w_out, w_up, w_down, norm_gains, norm_shifts = params
    row_count, model_width = hidden.shape
    hidden_low = hidden.astype(jnp.bfloat16)
    projected = forward_product(hidden_low, w_proj)
    self_term = projected[:, :model_width]
    dest_term = projected[:, 2 * model_width : 3 * model_width]
    source_rows = jnp.concatenate(
        [projected[:, model_width : 2 * model_width], projected[:, 3 * model_width :]], 1
    ).astype(jnp.bfloat16)
    incoming = exchange_sources(source_rows[halo_send])
    extended = jnp.concatenate([source_rows, incoming], 0)
    edge_rows = extended[edge_src].astype(jnp.float32)
    source_b = edge_rows[:, :model_width]
    source_e = edge_rows[:, model_width:]
    edge_proj = forward_product(edge_feat, w_edge)
    gating = jax.nn.sigmoid(dest_term[edge_dst] + source_e + edge_proj)
    numerator = jax.ops.segment_sum(gating * source_b, edge_dst, row_count)
    denominator = jax.ops.segment_sum(gating, edge_dst, row_count)
    message = self_term + numerator / (denominator + GATE_EPS)
    normed_one, standard_one, inv_one = normalize(
        message, norm_gains[0], norm_shifts[0], node_total
    )
    local_out = hidden + jax.nn.silu(normed_one)
    qkv_low = forward_product(hidden_low, w_qkv).astype(jnp.bfloat16)
    query_rows = qkv_low[:, :model_width]
    key_rows = qkv_low[:, model_width : 2 * model_width]
    value_rows = qkv_low[:, 2 * model_width :]
    attn_raw, log_sum = attend_forward(query_rows, key_rows, value_rows, local_graphs, group_graphs)
    attn_low = attn_raw.reshape(row_count, model_width).astype(jnp.bfloat16)
    attn_proj = forward_product(attn_low, w_out)
    normed_two, standard_two, inv_two = normalize(
        hidden + attn_proj, norm_gains[1], norm_shifts[1], node_total
    )
    mixed = local_out + normed_two
    mixed_low = mixed.astype(jnp.bfloat16)
    up_proj = forward_product(mixed_low, w_up)
    activated = jax.nn.silu(up_proj).astype(jnp.bfloat16)
    down_proj = forward_product(activated, w_down)
    normed_three, standard_three, inv_three = normalize(
        mixed + down_proj, norm_gains[2], norm_shifts[2], node_total
    )
    saved = (
        hidden_low,
        source_b,
        gating,
        numerator,
        denominator,
        normed_one,
        standard_one,
        inv_one,
        query_rows,
        key_rows,
        value_rows,
        attn_raw,
        log_sum,
        attn_low,
        standard_two,
        inv_two,
        mixed_low,
        up_proj,
        activated,
        standard_three,
        inv_three,
    )
    return (normed_three, saved)


def layer_backward(
    grad_out,
    params,
    saved,
    edge_feat,
    edge_src,
    edge_dst,
    halo_send,
    local_graphs,
    group_graphs,
    node_total,
):
    w_proj, w_edge, w_qkv, w_out, w_up, w_down, norm_gains, norm_shifts = params
    (
        hidden_low,
        source_b,
        gating,
        numerator,
        denominator,
        normed_one,
        standard_one,
        inv_one,
        query_rows,
        key_rows,
        value_rows,
        attn_raw,
        log_sum,
        attn_low,
        standard_two,
        inv_two,
        mixed_low,
        up_proj,
        activated,
        standard_three,
        inv_three,
    ) = saved
    row_count, model_width = grad_out.shape
    grad_three, gain_three, shift_three = normalize_back(
        grad_out, standard_three, inv_three, norm_gains[2], node_total
    )
    down_grad = grad_three.astype(jnp.bfloat16)
    grad_w_down = outer_product(activated, down_grad)
    up_grad = (times_transposed(down_grad, w_down) * silu_slope_plain(up_proj)).astype(jnp.bfloat16)
    grad_w_up = outer_product(mixed_low, up_grad)
    grad_mixed = grad_three + times_transposed(up_grad, w_up)
    grad_two, gain_two, shift_two = normalize_back(
        grad_mixed, standard_two, inv_two, norm_gains[1], node_total
    )
    out_grad = grad_two.astype(jnp.bfloat16)
    grad_w_out = outer_product(attn_low, out_grad)
    attn_grad = times_transposed(out_grad, w_out).astype(jnp.bfloat16)
    grad_query, grad_key, grad_value = attend_backward(
        query_rows, key_rows, value_rows, attn_grad, attn_raw, log_sum, local_graphs, group_graphs
    )
    qkv_grad = jnp.concatenate([grad_query, grad_key, grad_value], 1).astype(jnp.bfloat16)
    grad_w_qkv = outer_product(hidden_low, qkv_grad)
    grad_message, gain_one, shift_one = normalize_back(
        grad_mixed * silu_slope_plain(normed_one), standard_one, inv_one, norm_gains[0], node_total
    )
    shifted = denominator + GATE_EPS
    grad_numer = grad_message / shifted
    grad_denom = -grad_message * numerator / (shifted * shifted)
    numer_edge = grad_numer[edge_dst]
    grad_gate = numer_edge * source_b + grad_denom[edge_dst]
    grad_pre_edge = grad_gate * gating * (1.0 - gating)
    edge_grad = grad_pre_edge.astype(jnp.bfloat16)
    grad_w_edge = outer_product(edge_feat, edge_grad)
    grad_dest = jax.ops.segment_sum(grad_pre_edge, edge_dst, row_count)
    grad_extended = jax.ops.segment_sum(
        jnp.concatenate([numer_edge * gating, grad_pre_edge], 1),
        edge_src,
        row_count + halo_send.shape[0],
    )
    returned = return_sources(grad_extended[row_count:])
    grad_source = grad_extended[:row_count].at[halo_send].add(returned)
    proj_grad = jnp.concatenate(
        [grad_message, grad_source[:, :model_width], grad_dest, grad_source[:, model_width:]], 1
    ).astype(jnp.bfloat16)
    grad_w_proj = outer_product(hidden_low, proj_grad)
    grad_hidden = (
        grad_mixed
        + grad_two
        + times_transposed(proj_grad, w_proj)
        + times_transposed(qkv_grad, w_qkv)
    )
    weight_grads = (grad_w_proj, grad_w_edge, grad_w_qkv, grad_w_out, grad_w_up, grad_w_down)
    return (
        grad_hidden,
        weight_grads,
        jnp.stack([gain_one, gain_two, gain_three]),
        jnp.stack([shift_one, shift_two, shift_three]),
    )


def per_device(
    node_input,
    edge_feat,
    graph_ids,
    edge_src,
    edge_dst,
    halo_send,
    w_proj,
    w_edge,
    w_qkv,
    w_out,
    w_up,
    w_down,
    norm_gain,
    norm_shift,
    cotangent,
):
    group_graphs = lax.all_gather(graph_ids, "nodes", axis=0, tiled=True)
    node_total = node_input.shape[0] * lax.axis_size("nodes") * lax.axis_size("rep")
    layer_count = w_proj.shape[0]
    layer_params = [
        (
            w_proj[layer_index],
            w_edge[layer_index],
            w_qkv[layer_index],
            w_out[layer_index],
            w_up[layer_index],
            w_down[layer_index],
            norm_gain[layer_index],
            norm_shift[layer_index],
        )
        for layer_index in range(layer_count)
    ]
    hidden = node_input.astype(jnp.float32)
    saved_all = []
    for layer_index in range(layer_count):
        hidden, saved = layer_forward(
            hidden,
            layer_params[layer_index],
            edge_feat,
            edge_src,
            edge_dst,
            halo_send,
            graph_ids,
            group_graphs,
            node_total,
        )
        saved_all.append(saved)
    grad_hidden = cotangent.astype(jnp.float32)
    weight_parts = [None] * layer_count
    gain_parts = [None] * layer_count
    shift_parts = [None] * layer_count
    for layer_index in range(layer_count - 1, -1, -1):
        (
            grad_hidden,
            weight_parts[layer_index],
            gain_parts[layer_index],
            shift_parts[layer_index],
        ) = layer_backward(
            grad_hidden,
            layer_params[layer_index],
            saved_all[layer_index],
            edge_feat,
            edge_src,
            edge_dst,
            halo_send,
            graph_ids,
            group_graphs,
            node_total,
        )
    proj_local = jnp.stack([weight_parts[layer_index][0] for layer_index in range(layer_count)])
    edge_local = jnp.stack([weight_parts[layer_index][1] for layer_index in range(layer_count)])
    qkv_local = jnp.stack([weight_parts[layer_index][2] for layer_index in range(layer_count)])
    out_local = jnp.stack([weight_parts[layer_index][3] for layer_index in range(layer_count)])
    up_local = jnp.stack([weight_parts[layer_index][4] for layer_index in range(layer_count)])
    down_local = jnp.stack([weight_parts[layer_index][5] for layer_index in range(layer_count)])
    grad_proj, grad_edge, grad_qkv, grad_out, grad_up, grad_down = lax.psum(
        (proj_local, edge_local, qkv_local, out_local, up_local, down_local), ("nodes", "rep")
    )
    return (
        hidden,
        grad_hidden,
        grad_proj,
        grad_edge,
        grad_qkv,
        grad_out,
        grad_up,
        grad_down,
        jnp.stack(gain_parts),
        jnp.stack(shift_parts),
    )


def solution(mesh):
    in_specs = (
        P(("rep", "nodes"), None),
        P(("rep", "nodes"), None),
        P(("rep", "nodes")),
        P(("rep", "nodes")),
        P(("rep", "nodes")),
        P(("rep", "nodes")),
        P(),
        P(),
        P(),
        P(),
        P(),
        P(),
        P(),
        P(),
        P(("rep", "nodes"), None),
    )
    out_specs = (
        P(("rep", "nodes"), None),
        P(("rep", "nodes"), None),
        P(),
        P(),
        P(),
        P(),
        P(),
        P(),
        P(),
        P(),
    )
    N, M = mesh.shape["nodes"], mesh.shape["rep"]
    fused = N in (4, 8) and M % 2 == 0 and 512 % (16 * N * M) == 0
    return jax.shard_map(
        functools.partial(fused_device, N, M) if fused else per_device,
        mesh=mesh, in_specs=in_specs, out_specs=out_specs, check_vma=False,
    )
```

profile of v0, /device:TPU:1, one launch (start us, length us, event | category | flops | bytes accessed | tf_op | source)
XLA Modules:
  0.0 165.4 jit_solution(9666633665489650316)
XLA Ops:
  0.6 159.0 %layers.1 = (f32[192,256]{1,0:T(8,128)}, f32[192,256]{1,0:T(8,128)}, bf16[2560,128]{1,0:T(8,128)(2,1)}, bf16[2560,128]{1,0:T(8,128)(2,1)}, bf16[1536,128]{1,0:T(...) custom-call(bf16[192,256]{1,0:T(8,128)(2,1)} %args_0_.4, ...), custom_call_target="tpu_custom_call" | custom-call | tf_op jit(solution)/shard_map/layers/pallas_call | solution.py:950
  159.7 5.5 %gradients.1 = (f32[192,256]{1,0:T(8,128)}, f32[192,256]{1,0:T(8,128)}, f32[2,256,1024]{2,1,0:T(8,128)}, f32[2,256,256]{2,1,0:T(8,128)}, f32[2,256,768]{2,1,0:T(...) custom-call(f32[192,256]{1,0:T(8,128)} %get-tuple-element.31.act_h, ...), custom_call_target="tpu_custom_call" | custom-call | tf_op jit(solution)/shard_map/gradients/pallas_call | solution.py:963
where the time goes:
time: 166 us; the launch traced here: 165 us
  Pallas kernels  165 us (99%)
    pallas_call x1, Pallas kernels, fused_device(): pl.pallas_call(functools.partial(kernel, N, M, L, tuple(names)), out_shap...  159 us
    pallas_call x1, Pallas kernels, fused_device(): pl.pallas_call(finish_kernel, out_shape=[rows, rows, *weights, norm, norm...  5.52 us

commit v1 on v0

--- a/solution.py
+++ b/solution.py
@@ -18,11 +18,11 @@
 SYNCS = 12
 STRIP = 32
 GROUPS = (
-    ("early", 1, 0, 2560, ("core", "y", "nodes")),
-    ("conv", 1, 0, 2560, ("core", "y", "nodes")),
-    ("qkv", 1, 0, 1536, ("core", "y", "nodes")),
+    ("early", 1, 0, 2560, ("core", "y", "x", "z")),
+    ("conv", 1, 0, 2560, ("core", "y", "x", "z")),
+    ("qkv", 1, 0, 1536, ("core", "y", "x", "z")),
     ("early", 0, 0, 2560, ("core", "x", "y", "z")),
-    ("conv", 0, 0, 2560, ("core", "y", "nodes")),
+    ("conv", 0, 0, 2560, ("core", "y", "x", "z")),
     ("qkv", 0, 0, 1024, ("rep", "nodes")),
     ("qkv", 0, 1024, 512, ("nodes", "rep")),
 )
@@ -799,7 +799,7 @@
         first, last = b == 0, b == L - 1
         k = 3 * L + 1 + 2 * b
         back_feed_forward(l, k)
-        when(last, *steps((E1, 3), (Q1, 2)))
+        when(last, *steps((E1, 3), (C1, 3), (Q1, 2)))
         back_norms(l, k)
         if first:
             when(True, *steps((E1, 0)))
@@ -818,23 +818,24 @@
             conv_weight_grads(l)
             when(True, *steps((C1, 0)))
         else:
-            when(True, *steps((C1, 3), (E1, 4), (E0, 0)))
+            when(True, *steps((E1, 4), (C1, 4), (Q1, 3), (E0, 0)))
             sync_wait(k + 1)
             back_convolution(l, k)
+            send_halo(l)
+            conv_weight_grads(l)
+            when(True, *steps((E0, 1), (C0, 0)))
             back_heads(l, 0, 0)
-            send_halo(l)
-            when(True, *steps((Q1, 3), (E1, 5), (C1, 4), (E0, 1)))
-            conv_weight_grads(l)
+            when(True, *steps((E1, 5), (C1, 5), (Q1, 4), (C0, 1)))
             back_heads(l, 0, 1)
             back_rows(l, 0)
-            when(True, *steps((C0, 0), (E0, 2), (Q1, 4), (E1, 6), (C1, 5)))
+            when(True, *steps((E0, 2), (E1, 6), (C1, 6), (Q1, 5)))
             back_heads(l, 1, 0)
-            when(True, *steps((C0, 1), (E0, 3), (Q1, 5), (C1, 6)))
+            when(True, *steps((E0, 3), (C0, 2), (E1, 7), (C1, 7), (Q1, 6)))
             for t in range(2, NZ):
                 pass_on(l, 0, t)
             back_heads(l, 1, 1)
             back_rows(l, 1)
-            when(True, *steps((C0, 2), (E0, 4), (Q1, 6)))
+            when(True, *steps((E0, 4), (C0, 3), (E1, 8), (C1, 8), (Q1, 7)))
         dqb = (r_.dqT[...].T * scale).astype(BF16)
         r_.dxo[...] += dot_nt(dqb, r_.wqkv[l, :, 0:D])
         at = put(r_.gs_qkv, l, 0, dot(r_.xeT[:, 0:R], dqb))
@@ -853,15 +854,15 @@
 
     for b in range(L):
         backward(b)
-    for step in steps((QK0, 0), (V0, 0), (E0, 5), (C0, 3), (V0, 1), (QK0, 1)):
+    for step in steps((QK0, 0), (V0, 0), (E0, 5), (C0, 4), (V0, 1), (QK0, 1), (Q1, 8)):
         step()
     r_.dy[...] = back_input(0)
     in_copy = pltpu.make_async_copy(r_.dy, r_.grad_in, r_.store.at[1])
     in_copy.start()
     for step in steps(
-        (E0, 6), (C0, 4), (V0, 2), (QK0, 2),
-        (E0, 7), (C0, 5), (V0, 3), (QK0, 3),
-        (E0, 8), (C0, 6), (V0, 4), (QK0, 4),
+        (E0, 6), (C0, 5), (V0, 2), (QK0, 2),
+        (E0, 7), (C0, 6), (V0, 3), (QK0, 3),
+        (E0, 8), (C0, 7), (V0, 4), (QK0, 4), (C0, 8),
     ):
         step()
     for l in range(L):

time: 166 us -> 162 us (0.976)
  Pallas kernels: 165 us -> 161 us
    pallas_call x1, Pallas kernels: 159 us -> 155 us  [fused_device(): pl.pallas_call(functools.partial(kernel, N, M, L, tuple(names)), out_shap...]
where the time goes in v1:
time: 162 us; the launch traced here: 161 us
  Pallas kernels  161 us (99%)
    pallas_call x1, Pallas kernels, fused_device(): pl.pallas_call(functools.partial(kernel, N, M, L, tuple(names)), out_shap...  155 us
    pallas_call x1, Pallas kernels, fused_device(): pl.pallas_call(finish_kernel, out_shape=[rows, rows, *weights, norm, norm...  5.52 us

profile of v1, /device:TPU:1, one launch (start us, length us, event | category | flops | bytes accessed | tf_op | source)
XLA Modules:
  0.0 161.4 jit_solution(13543539898062453836)
XLA Ops:
  0.6 155.0 %layers.1 = (f32[192,256]{1,0:T(8,128)}, f32[192,256]{1,0:T(8,128)}, bf16[2560,128]{1,0:T(8,128)(2,1)}, bf16[2560,128]{1,0:T(8,128)(2,1)}, bf16[1536,128]{1,0:T(...) custom-call(bf16[192,256]{1,0:T(8,128)(2,1)} %args_0_.4, ...), custom_call_target="tpu_custom_call" | custom-call | tf_op jit(solution)/shard_map/layers/pallas_call | solution.py:951
  155.7 5.5 %gradients.1 = (f32[192,256]{1,0:T(8,128)}, f32[192,256]{1,0:T(8,128)}, f32[2,256,1024]{2,1,0:T(8,128)}, f32[2,256,256]{2,1,0:T(8,128)}, f32[2,256,768]{2,1,0:T(...) custom-call(f32[192,256]{1,0:T(8,128)} %get-tuple-element.31.act_h, ...), custom_call_target="tpu_custom_call" | custom-call | tf_op jit(solution)/shard_map/gradients/pallas_call | solution.py:964

commit v2 on v1

--- a/solution.py
+++ b/solution.py
@@ -799,7 +799,7 @@
         first, last = b == 0, b == L - 1
         k = 3 * L + 1 + 2 * b
         back_feed_forward(l, k)
-        when(last, *steps((E1, 3), (C1, 3), (Q1, 2)))
+        when(last, *steps((E1, 4), (C1, 4), (Q1, 2)))
         back_norms(l, k)
         if first:
             when(True, *steps((E1, 0)))
@@ -811,46 +811,48 @@
             back_convolution(l, k)
             send_halo(l)
             pass_on(l, 0, 2)
+            conv_weight_grads(l)
+            when(True, *steps((C1, 0)))
             back_heads(l, 1, 0)
             pass_on(l, 0, 3)
+            when(True, *steps((C1, 1)))
             back_heads(l, 1, 1)
             back_rows(l, 1)
-            conv_weight_grads(l)
-            when(True, *steps((C1, 0)))
         else:
-            when(True, *steps((E1, 4), (C1, 4), (Q1, 3), (E0, 0)))
+            when(True, *steps((E1, 5), (C1, 5), (Q1, 3), (E0, 0)))
             sync_wait(k + 1)
             back_convolution(l, k)
             send_halo(l)
+            when(True, *steps((E0, 1)))
             conv_weight_grads(l)
-            when(True, *steps((E0, 1), (C0, 0)))
+            when(True, *steps((C0, 0), (E1, 6), (C1, 6), (Q1, 4)))
             back_heads(l, 0, 0)
-            when(True, *steps((E1, 5), (C1, 5), (Q1, 4), (C0, 1)))
+            when(True, *steps((C0, 1)))
             back_heads(l, 0, 1)
             back_rows(l, 0)
-            when(True, *steps((E0, 2), (E1, 6), (C1, 6), (Q1, 5)))
+            when(True, *steps((E0, 2), (E1, 7), (C1, 7), (Q1, 5)))
             back_heads(l, 1, 0)
-            when(True, *steps((E0, 3), (C0, 2), (E1, 7), (C1, 7), (Q1, 6)))
+            when(True, *steps((E0, 3), (C0, 2), (E1, 8), (C1, 8), (Q1, 6)))
             for t in range(2, NZ):
                 pass_on(l, 0, t)
             back_heads(l, 1, 1)
             back_rows(l, 1)
-            when(True, *steps((E0, 4), (C0, 3), (E1, 8), (C1, 8), (Q1, 7)))
+            when(True, *steps((E0, 4), (C0, 3), (Q1, 7)))
         dqb = (r_.dqT[...].T * scale).astype(BF16)
         r_.dxo[...] += dot_nt(dqb, r_.wqkv[l, :, 0:D])
         at = put(r_.gs_qkv, l, 0, dot(r_.xeT[:, 0:R], dqb))
         put(r_.gs_qkv, l, at, r_.gkv[...].T)
         if first:
-            when(True, *steps((Q1, 0), (C1, 1)))
+            when(True, *steps((Q1, 0)))
             dx = back_input(l)
             r_.dy[...] = dx
             below = L - 2
             sync_start(SYNCS - 1, col_sum(dx), col_sum(dx * r_.z2[below]))
-            when(True, *steps((E1, 2), (Q1, 1)))
+            when(True, *steps((E1, 2), (C1, 2), (Q1, 1)))
             s2, g2 = sync_sums(SYNCS - 1)
             r_.gshift[below, 2:3] = s2
             r_.ggain[below, 2:3] = g2
-            when(True, *steps((C1, 2)))
+            when(True, *steps((E1, 3), (C1, 3)))
 
     for b in range(L):
         backward(b)

time: 162 us -> 163 us (level)
  no operation moved by 1% of the time
where the time goes in v2:
time: 163 us
  Pallas kernels  162 us (99%)
    pallas_call x1, Pallas kernels, fused_device(): pl.pallas_call(functools.partial(kernel, N, M, L, tuple(names)), out_shap...  156 us
    pallas_call x1, Pallas kernels, fused_device(): pl.pallas_call(finish_kernel, out_shape=[rows, rows, *weights, norm, norm...  5.52 us

profile of v2, /device:TPU:1, one launch (start us, length us, event | category | flops | bytes accessed | tf_op | source)
XLA Modules:
  0.0 162.7 jit_solution(6347330350918562663)
XLA Ops:
  0.6 156.4 %layers.1 = (f32[192,256]{1,0:T(8,128)}, f32[192,256]{1,0:T(8,128)}, bf16[2560,128]{1,0:T(8,128)(2,1)}, bf16[2560,128]{1,0:T(8,128)(2,1)}, bf16[1536,128]{1,0:T(...) custom-call(bf16[192,256]{1,0:T(8,128)(2,1)} %args_0_.4, ...), custom_call_target="tpu_custom_call" | custom-call | tf_op jit(solution)/shard_map/layers/pallas_call | solution.py:953
  157.0 5.5 %gradients.1 = (f32[192,256]{1,0:T(8,128)}, f32[192,256]{1,0:T(8,128)}, f32[2,256,1024]{2,1,0:T(8,128)}, f32[2,256,256]{2,1,0:T(8,128)}, f32[2,256,768]{2,1,0:T(...) custom-call(f32[192,256]{1,0:T(8,128)} %get-tuple-element.31.act_h, ...), custom_call_target="tpu_custom_call" | custom-call | tf_op jit(solution)/shard_map/gradients/pallas_call | solution.py:966

commit v3 on v2

--- a/solution.py
+++ b/solution.py
@@ -827,17 +827,17 @@
             conv_weight_grads(l)
             when(True, *steps((C0, 0), (E1, 6), (C1, 6), (Q1, 4)))
             back_heads(l, 0, 0)
-            when(True, *steps((C0, 1)))
+            when(True, *steps((E0, 2), (C0, 1)))
             back_heads(l, 0, 1)
             back_rows(l, 0)
-            when(True, *steps((E0, 2), (E1, 7), (C1, 7), (Q1, 5)))
+            when(True, *steps((E0, 3), (C0, 2), (E1, 7), (C1, 7), (Q1, 5)))
             back_heads(l, 1, 0)
-            when(True, *steps((E0, 3), (C0, 2), (E1, 8), (C1, 8), (Q1, 6)))
+            when(True, *steps((E0, 4), (C0, 3), (E1, 8), (C1, 8), (Q1, 6)))
             for t in range(2, NZ):
                 pass_on(l, 0, t)
             back_heads(l, 1, 1)
             back_rows(l, 1)
-            when(True, *steps((E0, 4), (C0, 3), (Q1, 7)))
+            when(True, *steps((E0, 5), (C0, 4), (Q1, 7)))
         dqb = (r_.dqT[...].T * scale).astype(BF16)
         r_.dxo[...] += dot_nt(dqb, r_.wqkv[l, :, 0:D])
         at = put(r_.gs_qkv, l, 0, dot(r_.xeT[:, 0:R], dqb))
@@ -856,15 +856,15 @@
 
     for b in range(L):
         backward(b)
-    for step in steps((QK0, 0), (V0, 0), (E0, 5), (C0, 4), (V0, 1), (QK0, 1), (Q1, 8)):
+    for step in steps((QK0, 0), (V0, 0), (E0, 6), (C0, 5), (Q1, 8), (V0, 1), (QK0, 1)):
         step()
     r_.dy[...] = back_input(0)
     in_copy = pltpu.make_async_copy(r_.dy, r_.grad_in, r_.store.at[1])
     in_copy.start()
     for step in steps(
-        (E0, 6), (C0, 5), (V0, 2), (QK0, 2),
-        (E0, 7), (C0, 6), (V0, 3), (QK0, 3),
-        (E0, 8), (C0, 7), (V0, 4), (QK0, 4), (C0, 8),
+        (C0, 6), (E0, 7), (V0, 2), (QK0, 2),
+        (C0, 7), (E0, 8), (V0, 3), (QK0, 3),
+        (C0, 8), (V0, 4), (QK0, 4),
     ):
         step()
     for l in range(L):

time: 163 us -> 163 us (level)
  no operation moved by 1% of the time
where the time goes in v3:
time: 163 us
  Pallas kernels  162 us (99%)
    pallas_call x1, Pallas kernels, fused_device(): pl.pallas_call(functools.partial(kernel, N, M, L, tuple(names)), out_shap...  157 us
    pallas_call x1, Pallas kernels, fused_device(): pl.pallas_call(finish_kernel, out_shape=[rows, rows, *weights, norm, norm...  5.52 us

profile of v3, /device:TPU:1, one launch (start us, length us, event | category | flops | bytes accessed | tf_op | source)
XLA Modules:
  0.0 163.1 jit_solution(6773825887790671897)
XLA Ops:
  0.6 156.8 %layers.1 = (f32[192,256]{1,0:T(8,128)}, f32[192,256]{1,0:T(8,128)}, bf16[2560,128]{1,0:T(8,128)(2,1)}, bf16[2560,128]{1,0:T(8,128)(2,1)}, bf16[1536,128]{1,0:T(...) custom-call(bf16[192,256]{1,0:T(8,128)(2,1)} %args_0_.4, ...), custom_call_target="tpu_custom_call" | custom-call | tf_op jit(solution)/shard_map/layers/pallas_call | solution.py:953
  157.4 5.5 %gradients.1 = (f32[192,256]{1,0:T(8,128)}, f32[192,256]{1,0:T(8,128)}, f32[2,256,1024]{2,1,0:T(8,128)}, f32[2,256,256]{2,1,0:T(8,128)}, f32[2,256,768]{2,1,0:T(...) custom-call(f32[192,256]{1,0:T(8,128)} %get-tuple-element.31.act_h, ...), custom_call_target="tpu_custom_call" | custom-call | tf_op jit(solution)/shard_map/gradients/pallas_call | solution.py:966

commit v4 on v3

--- a/solution.py
+++ b/solution.py
@@ -22,7 +22,7 @@
     ("conv", 1, 0, 2560, ("core", "y", "x", "z")),
     ("qkv", 1, 0, 1536, ("core", "y", "x", "z")),
     ("early", 0, 0, 2560, ("core", "x", "y", "z")),
-    ("conv", 0, 0, 2560, ("core", "y", "x", "z")),
+    ("conv", 0, 0, 2560, ("core", "x", "y", "z")),
     ("qkv", 0, 0, 1024, ("rep", "nodes")),
     ("qkv", 0, 1024, 512, ("nodes", "rep")),
 )

time: 163 us -> 162 us (level)
  no operation moved by 1% of the time
where the time goes in v4:
time: 162 us
  Pallas kernels  161 us (99%)
    pallas_call x1, Pallas kernels, fused_device(): pl.pallas_call(functools.partial(kernel, N, M, L, tuple(names)), out_shap...  155 us
    pallas_call x1, Pallas kernels, fused_device(): pl.pallas_call(finish_kernel, out_shape=[rows, rows, *weights, norm, norm...  5.52 us

profile of v4, /device:TPU:1, one launch (start us, length us, event | category | flops | bytes accessed | tf_op | source)
XLA Modules:
  0.0 161.9 jit_solution(13477012651491991286)
XLA Ops:
  0.6 155.5 %layers.1 = (f32[192,256]{1,0:T(8,128)}, f32[192,256]{1,0:T(8,128)}, bf16[2560,128]{1,0:T(8,128)(2,1)}, bf16[2560,128]{1,0:T(8,128)(2,1)}, bf16[1536,128]{1,0:T(...) custom-call(bf16[192,256]{1,0:T(8,128)(2,1)} %args_0_.4, ...), custom_call_target="tpu_custom_call" | custom-call | tf_op jit(solution)/shard_map/layers/pallas_call | solution.py:953
  156.2 5.5 %gradients.1 = (f32[192,256]{1,0:T(8,128)}, f32[192,256]{1,0:T(8,128)}, f32[2,256,1024]{2,1,0:T(8,128)}, f32[2,256,256]{2,1,0:T(8,128)}, f32[2,256,768]{2,1,0:T(...) custom-call(f32[192,256]{1,0:T(8,128)} %get-tuple-element.31.act_h, ...), custom_call_target="tpu_custom_call" | custom-call | tf_op jit(solution)/shard_map/gradients/pallas_call | solution.py:966

commit v5 on v4

--- a/solution.py
+++ b/solution.py
@@ -799,7 +799,7 @@
         first, last = b == 0, b == L - 1
         k = 3 * L + 1 + 2 * b
         back_feed_forward(l, k)
-        when(last, *steps((E1, 4), (C1, 4), (Q1, 2)))
+        when(last, *steps((E1, 4), (C1, 3), (Q1, 2)))
         back_norms(l, k)
         if first:
             when(True, *steps((E1, 0)))
@@ -807,52 +807,51 @@
             back_heads(l, 0, 1)
             back_rows(l, 0)
             when(True, *steps((E1, 1)))
+            back_heads(l, 1, 0)
+            pass_on(l, 0, 2)
+            back_heads(l, 1, 1)
+            back_rows(l, 1)
+            pass_on(l, 0, 3)
             sync_wait(k + 1)
             back_convolution(l, k)
             send_halo(l)
-            pass_on(l, 0, 2)
             conv_weight_grads(l)
             when(True, *steps((C1, 0)))
-            back_heads(l, 1, 0)
-            pass_on(l, 0, 3)
-            when(True, *steps((C1, 1)))
-            back_heads(l, 1, 1)
-            back_rows(l, 1)
         else:
-            when(True, *steps((E1, 5), (C1, 5), (Q1, 3), (E0, 0)))
+            when(True, *steps((E1, 5), (C1, 4), (Q1, 3), (E0, 0)))
             sync_wait(k + 1)
             back_convolution(l, k)
             send_halo(l)
             when(True, *steps((E0, 1)))
             conv_weight_grads(l)
-            when(True, *steps((C0, 0), (E1, 6), (C1, 6), (Q1, 4)))
+            when(True, *steps((C0, 0), (E1, 6), (C1, 5), (Q1, 4)))
             back_heads(l, 0, 0)
             when(True, *steps((E0, 2), (C0, 1)))
             back_heads(l, 0, 1)
             back_rows(l, 0)
-            when(True, *steps((E0, 3), (C0, 2), (E1, 7), (C1, 7), (Q1, 5)))
+            when(True, *steps((E0, 3), (C0, 2), (E1, 7), (C1, 6), (Q1, 5)))
             back_heads(l, 1, 0)
-            when(True, *steps((E0, 4), (C0, 3), (E1, 8), (C1, 8), (Q1, 6)))
+            when(True, *steps((E0, 4), (C0, 3), (E1, 8), (C1, 7), (Q1, 6)))
             for t in range(2, NZ):
                 pass_on(l, 0, t)
             back_heads(l, 1, 1)
             back_rows(l, 1)
-            when(True, *steps((E0, 5), (C0, 4), (Q1, 7)))
+            when(True, *steps((E0, 5), (C0, 4), (C1, 8), (Q1, 7)))
         dqb = (r_.dqT[...].T * scale).astype(BF16)
         r_.dxo[...] += dot_nt(dqb, r_.wqkv[l, :, 0:D])
         at = put(r_.gs_qkv, l, 0, dot(r_.xeT[:, 0:R], dqb))
         put(r_.gs_qkv, l, at, r_.gkv[...].T)
         if first:
-            when(True, *steps((Q1, 0)))
+            when(True, *steps((Q1, 0), (C1, 1)))
             dx = back_input(l)
             r_.dy[...] = dx
             below = L - 2
             sync_start(SYNCS - 1, col_sum(dx), col_sum(dx * r_.z2[below]))
-            when(True, *steps((E1, 2), (C1, 2), (Q1, 1)))
+            when(True, *steps((E1, 2), (Q1, 1)))
             s2, g2 = sync_sums(SYNCS - 1)
             r_.gshift[below, 2:3] = s2
             r_.ggain[below, 2:3] = g2
-            when(True, *steps((E1, 3), (C1, 3)))
+            when(True, *steps((E1, 3), (C1, 2)))
 
     for b in range(L):
         backward(b)

time: 162 us -> 160 us (0.988)
  Pallas kernels: 161 us -> 159 us
    pallas_call x1, Pallas kernels: 155 us -> 153 us  [fused_device(): pl.pallas_call(functools.partial(kernel, N, M, L, tuple(names)), out_shap...]
where the time goes in v5:
time: 160 us; the launch traced here: 159 us
  Pallas kernels  159 us (99%)
    pallas_call x1, Pallas kernels, fused_device(): pl.pallas_call(functools.partial(kernel, N, M, L, tuple(names)), out_shap...  153 us
    pallas_call x1, Pallas kernels, fused_device(): pl.pallas_call(finish_kernel, out_shape=[rows, rows, *weights, norm, norm...  5.52 us

profile of v5, /device:TPU:1, one launch (start us, length us, event | category | flops | bytes accessed | tf_op | source)
XLA Modules:
  0.0 159.4 jit_solution(4142730321745879779)
XLA Ops:
  0.6 153.1 %layers.1 = (f32[192,256]{1,0:T(8,128)}, f32[192,256]{1,0:T(8,128)}, bf16[2560,128]{1,0:T(8,128)(2,1)}, bf16[2560,128]{1,0:T(8,128)(2,1)}, bf16[1536,128]{1,0:T(...) custom-call(bf16[192,256]{1,0:T(8,128)(2,1)} %args_0_.4, ...), custom_call_target="tpu_custom_call" | custom-call | tf_op jit(solution)/shard_map/layers/pallas_call | solution.py:952
  153.7 5.5 %gradients.1 = (f32[192,256]{1,0:T(8,128)}, f32[192,256]{1,0:T(8,128)}, f32[2,256,1024]{2,1,0:T(8,128)}, f32[2,256,256]{2,1,0:T(8,128)}, f32[2,256,768]{2,1,0:T(...) custom-call(f32[192,256]{1,0:T(8,128)} %get-tuple-element.31.act_h, ...), custom_call_target="tpu_custom_call" | custom-call | tf_op jit(solution)/shard_map/gradients/pallas_call | solution.py:965
